TPU v7x, 32 devices: a whole 2x2x4 slice. The times are simulated.
32 devices in a mesh: groups: 2 (over y), fsdp: 4 (over z), dp: 2 (over x), pair: 2 (over core).
Axes of the slice: x: 2, y: 2, z: 4, core: 2. Of those that a mesh axis runs over, the one named last changes fastest.
Arguments:
- hidden_input: bfloat16 [4096, 8192], P(('groups', 'fsdp', 'dp', 'pair')), parts along dimension 0, may hold values from -6 to 6
- norm_gain_vector: float32 [8192], replicated, may hold values from 0.5 to 18, as said below
- value_matrix: bfloat16 [8192, 768], P('fsdp'), may hold values from -0.0625 to 0.0625
- adapter_down_map: bfloat16 [16384, 64], P(('groups', 'fsdp')), parts along dimension 0, may hold values from -0.0625 to 0.0625
- adapter_up_map: bfloat16 [128, 768], P('groups'), parts along dimension 0, may hold values from -5 to 5
- values_gradient: bfloat16 [4096, 768], P(('groups', 'fsdp', 'dp', 'pair')), parts along dimension 0, may hold values from -6 to 6
Outputs:
- grad_hidden: bfloat16 [4096, 8192], P(('groups', 'fsdp', 'dp', 'pair')), parts along dimension 0
- grad_down: float32 [16384, 64], P(('groups', 'fsdp')), parts along dimension 0
- grad_up: float32 [128, 768], P('groups'), parts along dimension 0
There are 2 independent parts, one for each index of `groups`. A program takes and returns all parts, laid end to end along the dimension named above; an argument that names none is the same for every part. Nothing has to cross between parts.
Inputs may be any that keep to these rules, and one draw needn't show every extreme that they name: `norm_gain_vector`: positive gains.
All inputs are finite; a program needn't handle non-finite values.
Results may differ from a plain program's by a relative error of at most 0.0085.
Values may be sent and summed in bfloat16 or wider, within the bound.
A program may use at most 64 MiB of HBM per device.

v0:
```python
import math
import jax
import jax.numpy as jnp
from jax import lax
from jax.sharding import PartitionSpec as P

MODEL_WIDTH = 8192
ADAPTER_RANK = 64
norm_eps = 1e-05
adapter_scale = 2.0


def contract_last(left, right):
    return lax.dot_general(
        left, right, (((1,), (1,)), ((), ())), preferred_element_type=jnp.float32
    )


def contract_leading(left, right):
    return lax.dot_general(
        left, right, (((0,), (0,)), ((), ())), preferred_element_type=jnp.float32
    )


def local(
    hidden_input, norm_gain_vector, value_matrix, adapter_down_map, adapter_up_map, values_gradient
):
    width = hidden_input.shape[1]
    stream = hidden_input.astype(jnp.float32)
    inv_rms = lax.rsqrt(jnp.mean(stream * stream, axis=1, keepdims=True) + norm_eps)
    normalized_input = (stream * inv_rms * norm_gain_vector).astype(jnp.bfloat16)
    upward_product = (
        adapter_scale
        * jnp.dot(values_gradient, adapter_up_map.T, preferred_element_type=jnp.float32)
    ).astype(jnp.bfloat16)
    every_values, every_upward = (
        lax.all_gather(values_gradient, "fsdp", axis=0, tiled=True),
        lax.all_gather(upward_product, "fsdp", axis=0, tiled=True),
    )
    columns = contract_last(every_values, value_matrix) + contract_last(
        every_upward, adapter_down_map
    )
    gradient_normalized = lax.all_to_all(
        columns.astype(jnp.bfloat16), "fsdp", split_axis=0, concat_axis=1, tiled=True
    )
    window = normalized_input
    latent_f = jnp.dot(
        window,
        lax.all_gather(adapter_down_map, "fsdp", axis=0, tiled=True),
        preferred_element_type=jnp.float32,
    )
    scaled = gradient_normalized.astype(jnp.float32) * norm_gain_vector
    grad_stream = inv_rms * scaled - stream * (inv_rms**3 / width) * jnp.sum(
        scaled * stream, axis=1, keepdims=True
    )
    latent_code = latent_f.astype(jnp.bfloat16)
    window = normalized_input
    down_shard = lax.psum_scatter(
        contract_leading(window, upward_product), "fsdp", scatter_dimension=0, tiled=True
    )
    up_portion = adapter_scale * contract_leading(latent_code, values_gradient)
    down_shard = lax.psum(down_shard, ("dp", "pair"))
    up_full = lax.psum(up_portion, ("fsdp", "dp", "pair"))
    total = lax.psum(jnp.sum(down_shard * down_shard), "fsdp") + jnp.sum(up_full * up_full)
    factor = jnp.minimum(1.0, 0.5 * math.sqrt(MODEL_WIDTH * ADAPTER_RANK) / jnp.sqrt(total))
    return (grad_stream.astype(jnp.bfloat16), factor * down_shard, factor * up_full)


def solution(mesh):
    return jax.shard_map(
        local,
        mesh=mesh,
        in_specs=(
            P(("groups", "fsdp", "dp", "pair"), None),
            P(),
            P("fsdp", None),
            P(("groups", "fsdp"), None),
            P("groups", None),
            P(("groups", "fsdp", "dp", "pair"), None),
        ),
        out_specs=(
            P(("groups", "fsdp", "dp", "pair"), None),
            P(("groups", "fsdp"), None),
            P("groups", None),
        ),
        check_vma=False,
    )
```

profile of v0, /device:TPU:0, one launch (start us, length us, event | category | flops | bytes accessed | tf_op | source)
XLA Modules:
  0.0 322.7 jit_solution(588120099054937987)
XLA Ops:
  7.2 0.0 copy-start
  7.2 0.0 reduce-scatter.2.cloned.1.call-start
  7.2 21.6 %all_gather.9 = bf16[512,768]{1,0:T(8,128)(2,1)S(1)} all-gather(bf16[128,768]{1,0:T(8,128)(2,1)} %param.11), channel_id=1, replica_groups=mesh['groups'=2,'fsdp'=4,'dp'=2,'pair'=2] {'fsdp'}, dimensions={0}, use_global_device_ids=true | all-gather | bytes 983040 | tf_op jit(solution)/shard_map/all_gather | solution.py:37
  28.9 1.2 fusion.7
  30.1 12.0 %all_gather.10 = bf16[512,64]{0,1:T(8,128)(2,1)S(1)} all-gather(bf16[128,64]{0,1:T(8,128)(2,1)S(1)} %fusion.7), channel_id=1, replica_groups=mesh['groups'=2,'fsdp'=4,'dp'=2,'pair'=2] {'fsdp'}, dimensions={0}, use_global_device_ids=true | all-gather | bytes 81920 | tf_op jit(solution)/shard_map/all_gather | solution.py:38
  42.0 0.0 copy-done
  42.1 0.0 copy-start.3
  42.1 1.8 fusion.13
  43.9 0.0 copy-done.3
  43.9 0.7 add_convert_fusion
  44.6 46.4 %all_to_all.13 = bf16[4,128,2048]{2,1,0:T(8,128)(2,1)S(1)} all-to-all(bf16[4,128,2048]{2,1,0:T(8,128)(2,1)S(1)} %bitcast.16), channel_id=1, replica_groups=mesh['groups'=2,'fsdp'=4,'dp'=2,'pair'=2] {'fsdp'}, dimensions={0} | all-to-all | bytes 4194304 | tf_op jit(solution)/shard_map/all_to_all | solution.py:43
  91.1 0.5 convert_bitcast_fusion
  91.6 0.0 copy-start.2
  91.6 0.0 copy-start.5
  91.6 0.5 copy.10
  92.1 0.0 copy-start.1
  92.1 1.9 copy-done.1
  94.0 0.0 copy-done.2
  94.0 0.0 copy-done.5
  94.0 1.2 fusion
  95.2 0.0 copy-start.4
  95.2 2.2 fusion.10
  97.4 0.0 reduce-scatter.2.cloned.1.call-update
  97.4 0.0 all-gather.2.cloned.1.call-start
  97.5 0.7 all-gather.2.cloned.1.call-update
  98.2 0.0 all-reduce.3.cloned.1.call-start
  98.2 42.3 %reduce-scatter.2.cloned.1.call-done = f32[2048,64]{0,1:T(8,128)} async-done(((f32[8192,64]{0,1:T(8,128)}), f32[2048,64]{0,1:T(8,128)}) %reduce-scatter.2.cloned.1.call-update) | async-done | bytes 524304 | tf_op jit(solution)/shard_map/reduce_scatter | solution.py:58
  140.5 0.0 all-reduce.3.cloned.1.call-update
  140.6 0.0 all-reduce.5.cloned.1.call-start
  140.6 28.9 %all-gather.2.cloned.1.call-done = bf16[8192,64]{0,1:T(8,128)(2,1)} async-done(((bf16[2048,64]{0,1:T(8,128)(2,1)}), bf16[8192,64]{0,1:T(8,128)(2,1)}) %all-gather.2.cloned.1.call-update) | async-done | bytes 1048592 | tf_op jit(solution)/shard_map/all_gather | solution.py:49
  169.5 0.0 copy-done.4
  169.5 3.5 %convolution_multiply_fusion = f32[64,768]{1,0:T(8,128)} fusion(bf16[128,768]{1,0:T(8,128)(2,1)S(1)} %copy-done.4, bf16[8192,64]{0,1:T(8,128)(2,1)} %all-gather.2.cloned.1.call-done, bf16[128,8192]{1,0:T(8,128)(2,1)} %param.6, f32[8192]{0:T(1024)S(1)} %copy-done.5, f32[128]{0:T(128)S(1)} %get-tuple-element.5), kind=kOutput, calls=%fused_computation.13 | convolution fusion | flops 151052288 | bytes 3572224 | tf_op jit(solution)/shard_map/dot_general | solution.py:20
  173.0 0.0 all-reduce.5.cloned.1.call-update
  173.1 5.3 %fusion.3 = bf16[128,8192]{1,0:T(8,128)(2,1)} fusion(bf16[128,8192]{1,0:T(8,128)(2,1)} %param.6, f32[128,8192]{1,0:T(8,128)} %bitcast.15, f32[128]{0:T(128)S(1)} %get-tuple-element.4, f32[128]{0:T(128)S(1)} %get-tuple-element.6, f32[8192]{0:T(1024)S(1)} %copy-done.5, f32[128]{0:T(128)S(1)} %get-tuple-element.5), kind=kLoop, calls=%fused_computation.7 | loop fusion | flops 7340032 | bytes 8422912 | tf_op jit(solution)/shard_map/convert_element_type | solution.py:66
  178.4 26.3 %all-reduce.3.cloned.1.call-done = f32[2048,64]{0,1:T(8,128)} async-done(((f32[2048,64]{0,1:T(8,128)}), f32[2048,64]{0,1:T(8,128)}) %all-reduce.3.cloned.1.call-update) | async-done | bytes 524304 | tf_op jit(solution)/shard_map/psum | solution.py:62
  204.7 1.8 multiply_reduce_fusion
  206.5 92.0 %all-reduce.5.cloned.1.call-done = f32[64,768]{1,0:T(8,128)} async-done(((f32[64,768]{1,0:T(8,128)}), f32[64,768]{1,0:T(8,128)}) %all-reduce.5.cloned.1.call-update) | async-done | bytes 196624 | tf_op jit(solution)/shard_map/psum | solution.py:63
  298.5 1.6 multiply_reduce_fusion.1
  300.1 11.2 %psum.22 = f32[]{:T(128)} all-reduce(f32[]{:T(128)} %multiply_reduce_fusion), channel_id=1, replica_groups=mesh['groups'=2,'fsdp'=4,'dp'=2,'pair'=2] {'fsdp'}, use_global_device_ids=true, to_apply=%region_5.0 | all-reduce | flops 1 | bytes 8 | tf_op jit(solution)/shard_map/psum | solution.py:64
  312.7 1.9 broadcast_multiply_fusion
  314.6 1.6 broadcast_multiply_fusion.1
  (1 shorter events, 0.0 us)
Async XLA Ops:
  7.2 34.9 %copy-start = (bf16[2048,768]{1,0:T(8,128)(2,1)S(1)}, bf16[2048,768]{1,0:T(8,128)(2,1)}, u32[]{:S(2)}) copy-start(bf16[2048,768]{1,0:T(8,128)(2,1)} %param.8) | copy-start | bytes 9437188
  7.2 133.4 %reduce-scatter.2.cloned.1.call-start = ((), (), s32[]{:S(2)}) async-start(), calls=%async_computation.2 | async-start | bytes 2621440 | tf_op jit(solution)/shard_map/reduce_scatter | solution.py:58
  42.1 1.8 copy-start.3
  91.6 2.5 copy-start.2
  91.6 2.4 copy-start.5
  92.1 1.9 copy-start.1
  95.2 74.3 %copy-start.4 = (bf16[128,768]{1,0:T(8,128)(2,1)S(1)}, bf16[128,768]{1,0:T(8,128)(2,1)}, u32[]{:S(2)}) copy-start(bf16[128,768]{1,0:T(8,128)(2,1)} %param.11) | copy-start | bytes 589828
  97.4 72.1 %all-gather.2.cloned.1.call-start = ((), (), s32[]{:S(2)}) async-start(), calls=%async_computation.4 | async-start | bytes 1310720 | tf_op jit(solution)/shard_map/all_gather | solution.py:49
  98.2 106.5 %all-reduce.3.cloned.1.call-start = ((), (), s32[]{:S(2)}) async-start(), calls=%async_computation.3 | async-start | bytes 1048576 | tf_op jit(solution)/shard_map/psum | solution.py:62
  140.6 157.9 %all-reduce.5.cloned.1.call-start = ((), (), s32[]{:S(2)}) async-start(), calls=%async_computation.5 | async-start | bytes 393216 | tf_op jit(solution)/shard_map/psum | solution.py:63
Sparse Core Ops, SparseCore 0:
  97.6 42.9 reduce-scatter.1
  142.2 27.2 all-gather.1
  172.0 32.6 all-reduce.2
  208.9 89.5 all-reduce.4
where the time goes:
time: 323 us
  waiting for transfers between devices  190 us (59%)
  blocking collectives  91.3 us (28%)
  between operations  15.2 us (5%)
  other arithmetic  13.9 us (4%)
  matrix products  9.43 us (3%)
    psum x1, waiting for transfers between devices, local(): up_full = lax.psum(up_portion, ('fsdp', 'dp', 'pair'))  92 us
    all_to_all x1, blocking collectives, local(): lax.all_to_all(columns.astype(jnp.bfloat16), 'fsdp', split_axis=0, concat...  46.4 us
    reduce_scatter x1, waiting for transfers between devices, local(): lax.psum_scatter(contract_leading(window, upward_product), 'fsdp', scatte...  42.3 us
    all_gather x1, waiting for transfers between devices, local(): lax.all_gather(adapter_down_map, 'fsdp', axis=0, tiled=True)  28.9 us
    psum x1, waiting for transfers between devices, local(): down_shard = lax.psum(down_shard, ('dp', 'pair'))  26.3 us
    all_gather x1, blocking collectives, local(): lax.all_gather(values_gradient, 'fsdp', axis=0, tiled=True)  21.6 us
    all_gather x1, blocking collectives, local(): lax.all_gather(upward_product, 'fsdp', axis=0, tiled=True)  12 us
    psum x1, blocking collectives, local(): lax.psum(jnp.sum(down_shard * down_shard), 'fsdp')  11.2 us
  transfers between devices with their start and end apart: 4, of which 4 were waited for; matrix products, arithmetic and copies ran while one was open for 3% of the time, Pallas kernels for 0%

commit v1 on v0

--- a/solution.py
+++ b/solution.py
@@ -8,6 +8,24 @@
 ADAPTER_RANK = 64
 norm_eps = 1e-05
 adapter_scale = 2.0
+
+
+def gather_around(shard, axis, dim):
+    ways, here, step = (lax.axis_size(axis), lax.axis_index(axis), shard.shape[dim])
+    shape = [n * ways if d == dim else n for d, n in enumerate(shard.shape)]
+    full = lax.dynamic_update_slice_in_dim(
+        jnp.zeros(shape, shard.dtype), shard, here * step, axis=dim
+    )
+    going_up = going_down = shard
+    for far in range(1, ways // 2 + 1):
+        going_up = lax.ppermute(going_up, axis, [(d, (d + 1) % ways) for d in range(ways)])
+        full = lax.dynamic_update_slice_in_dim(full, going_up, (here - far) % ways * step, axis=dim)
+        if 2 * far < ways:
+            going_down = lax.ppermute(going_down, axis, [(d, (d - 1) % ways) for d in range(ways)])
+            full = lax.dynamic_update_slice_in_dim(
+                full, going_down, (here + far) % ways * step, axis=dim
+            )
+    return full
 
 
 def contract_last(left, right):
@@ -34,7 +52,7 @@
         * jnp.dot(values_gradient, adapter_up_map.T, preferred_element_type=jnp.float32)
     ).astype(jnp.bfloat16)
     every_values, every_upward = (
-        lax.all_gather(values_gradient, "fsdp", axis=0, tiled=True),
+        gather_around(values_gradient, "fsdp", 0),
         lax.all_gather(upward_product, "fsdp", axis=0, tiled=True),
     )
     columns = contract_last(every_values, value_matrix) + contract_last(

time: 323 us -> 323 us (level)
  blocking collectives: 91.3 us -> 73.2 us
  starting transfers between devices: 0.16 us -> 6.51 us
  waiting for transfers between devices: 190 us -> 196 us
  matrix products: 9.43 us -> 14.5 us
    all_gather x1 -> x0, blocking collectives: 21.6 us -> none  [local(): lax.all_gather(values_gradient, 'fsdp', axis=0, tiled=True)]
    ppermute x0 -> x3, starting transfers between devices: none -> 6.36 us  [the longest x2 4.27 us: gather_around(): lax.ppermute(going_up, axis, [(d, (d + 1) % ways) for d in range(ways)])]
    ppermute x0 -> x3, waiting for transfers between devices: none -> 5.35 us  [the longest x2 5.35 us: gather_around(): lax.ppermute(going_up, axis, [(d, (d + 1) % ways) for d in range(ways)])]
    dot_general x2, matrix products: 2.55 us -> 7.65 us  [contract_last(): lax.dot_general(left, right, (((1,), (1,)), ((), ())), preferred_element_...]
  transfers between devices with their start and end apart: 4 -> 7, of which waited for: 4 -> 5; matrix products, arithmetic and copies ran while one was open for 3% -> 5% of each run, Pallas kernels for 0% -> 0%
where the time goes in v1:
time: 323 us; the launch traced here: 322 us
  waiting for transfers between devices  196 us (61%)
  blocking collectives  73.2 us (23%)
  between operations  15.2 us (5%)
  matrix products  14.5 us (4%)
  other arithmetic  13.9 us (4%)
  starting transfers between devices  6.51 us (2%)
  local copies, waits for them, and re-layouts  3.49 us (1%)
    psum x1, waiting for transfers between devices, local(): up_full = lax.psum(up_portion, ('fsdp', 'dp', 'pair'))  92 us
    all_to_all x1, blocking collectives, local(): lax.all_to_all(columns.astype(jnp.bfloat16), 'fsdp', split_axis=0, concat...  47.7 us
    reduce_scatter x1, waiting for transfers between devices, local(): lax.psum_scatter(contract_leading(window, upward_product), 'fsdp', scatte...  42.3 us
    all_gather x1, waiting for transfers between devices, local(): lax.all_gather(adapter_down_map, 'fsdp', axis=0, tiled=True)  28.9 us
    psum x1, waiting for transfers between devices, local(): down_shard = lax.psum(down_shard, ('dp', 'pair'))  26.3 us
    all_gather x1, blocking collectives, local(): lax.all_gather(upward_product, 'fsdp', axis=0, tiled=True)  14.3 us
    psum x1, blocking collectives, local(): lax.psum(jnp.sum(down_shard * down_shard), 'fsdp')  11.2 us
    dot_general x2, matrix products, contract_last(): lax.dot_general(left, right, (((1,), (1,)), ((), ())), preferred_element_...  7.65 us
  transfers between devices with their start and end apart: 7, of which 5 were waited for; matrix products, arithmetic and copies ran while one was open for 5% of the time, Pallas kernels for 0%

profile of v1, /device:TPU:0, one launch (start us, length us, event | category | flops | bytes accessed | tf_op | source)
XLA Modules:
  0.0 322.5 jit_solution(8233561451906112992)
XLA Ops:
  7.2 0.0 copy-start
  7.2 0.0 copy-start.3
  7.2 0.0 reduce-scatter.2.cloned.1.call-start
  7.2 3.1 collective-permute-start
  10.3 2.1 collective-permute-start.1
  12.4 1.2 fusion.7
  13.6 14.3 %all_gather.6 = bf16[512,64]{0,1:T(8,128)(2,1)S(1)} all-gather(bf16[128,64]{0,1:T(8,128)(2,1)S(1)} %fusion.7), channel_id=1, replica_groups=mesh['groups'=2,'fsdp'=4,'dp'=2,'pair'=2] {'fsdp'}, dimensions={0}, use_global_device_ids=true | all-gather | bytes 81920 | tf_op jit(solution)/shard_map/all_gather | solution.py:56
  27.9 3.6 %fusion.13 = f32[512,2048]{1,0:T(8,128)} fusion(bf16[512,64]{0,1:T(8,128)(2,1)S(1)} %all_gather.6, bf16[2048,64]{0,1:T(8,128)(2,1)} %param.9), kind=kOutput, calls=%fused_computation.29 | convolution fusion | flops 134217728 | bytes 4521984 | tf_op jit(solution)/shard_map/dot_general | solution.py:32
  31.5 0.1 broadcast_in_dim.2
  31.5 0.0 copy-done.3
  31.6 0.0 collective-permute-done
  31.6 1.2 collective-permute-start.2
  32.8 0.0 collective-permute-done.1
  32.8 0.9 constant_dynamic-update-slice_fusion.1
  33.7 5.3 %collective-permute-done.2 = bf16[128,768]{1,0:T(8,128)(2,1)S(1)} collective-permute-done((bf16[128,768]{1,0:T(8,128)(2,1)S(1)}, bf16[128,768]{1,0:T(8,128)(2,1)S(1)}, u32[]{:S(2)}, u32[]{:S(2)}) %collective-permute-start.2) | collective-permute-done | bytes 196640 | tf_op jit(solution)/shard_map/ppermute | solution.py:21
  39.1 0.0 copy-done
  39.1 4.1 %add_convert_fusion = bf16[512,2048]{1,0:T(8,128)(2,1)S(1)} fusion(f32[512,2048]{1,0:T(8,128)} %fusion.13, bf16[512,768]{1,0:T(8,128)(2,1)S(1)} %constant_dynamic-update-slice_fusion, bf16[2048,768]{1,0:T(8,128)(2,1)S(1)} %copy-done), kind=kOutput, calls=%fused_computation.12 | convolution fusion | flops 1612709888 | bytes 10223616 | tf_op jit(solution)/shard_map/dot_general | solution.py:32
  43.2 47.7 %all_to_all.13 = bf16[4,128,2048]{2,1,0:T(8,128)(2,1)S(1)} all-to-all(bf16[4,128,2048]{2,1,0:T(8,128)(2,1)S(1)} %bitcast.16), channel_id=1, replica_groups=mesh['groups'=2,'fsdp'=4,'dp'=2,'pair'=2] {'fsdp'}, dimensions={0} | all-to-all | bytes 4194304 | tf_op jit(solution)/shard_map/all_to_all | solution.py:61
  90.9 0.5 convert_bitcast_fusion
  91.4 0.0 copy-start.2
  91.4 0.0 copy-start.4
  91.5 0.5 copy.10
  91.9 0.0 copy-start.1
  92.0 1.9 copy-done.1
  93.9 0.0 copy-done.2
  93.9 0.0 copy-done.4
  93.9 1.2 fusion
  95.1 2.2 fusion.10
  97.2 0.0 reduce-scatter.2.cloned.1.call-update
  97.3 0.0 all-gather.2.cloned.1.call-start
  97.3 0.7 all-gather.2.cloned.1.call-update
  98.0 0.0 all-reduce.3.cloned.1.call-start
  98.1 42.3 %reduce-scatter.2.cloned.1.call-done = f32[2048,64]{0,1:T(8,128)} async-done(((f32[8192,64]{0,1:T(8,128)}), f32[2048,64]{0,1:T(8,128)}) %reduce-scatter.2.cloned.1.call-update) | async-done | bytes 524304 | tf_op jit(solution)/shard_map/reduce_scatter | solution.py:76
  140.3 0.0 all-reduce.3.cloned.1.call-update
  140.3 0.0 all-reduce.5.cloned.1.call-start
  140.4 28.9 %all-gather.2.cloned.1.call-done = bf16[8192,64]{0,1:T(8,128)(2,1)} async-done(((bf16[2048,64]{0,1:T(8,128)(2,1)}), bf16[8192,64]{0,1:T(8,128)(2,1)}) %all-gather.2.cloned.1.call-update) | async-done | bytes 1048592 | tf_op jit(solution)/shard_map/all_gather | solution.py:67
  169.3 3.5 %convolution_multiply_fusion = f32[64,768]{1,0:T(8,128)} fusion(bf16[128,768]{1,0:T(8,128)(2,1)S(1)} %copy-done.3, bf16[8192,64]{0,1:T(8,128)(2,1)} %all-gather.2.cloned.1.call-done, bf16[128,8192]{1,0:T(8,128)(2,1)} %param.6, f32[8192]{0:T(1024)S(1)} %copy-done.4, f32[128]{0:T(128)S(1)} %get-tuple-element.5), kind=kOutput, calls=%fused_computation.13 | convolution fusion | flops 151052288 | bytes 3572224 | tf_op jit(solution)/shard_map/dot_general | solution.py:38
  172.8 0.0 all-reduce.5.cloned.1.call-update
  172.8 5.3 %fusion.3 = bf16[128,8192]{1,0:T(8,128)(2,1)} fusion(bf16[128,8192]{1,0:T(8,128)(2,1)} %param.6, f32[128,8192]{1,0:T(8,128)} %bitcast.15, f32[128]{0:T(128)S(1)} %get-tuple-element.4, f32[128]{0:T(128)S(1)} %get-tuple-element.6, f32[8192]{0:T(1024)S(1)} %copy-done.4, f32[128]{0:T(128)S(1)} %get-tuple-element.5), kind=kLoop, calls=%fused_computation.7 | loop fusion | flops 7340032 | bytes 8422912 | tf_op jit(solution)/shard_map/convert_element_type | solution.py:84
  178.2 26.3 %all-reduce.3.cloned.1.call-done = f32[2048,64]{0,1:T(8,128)} async-done(((f32[2048,64]{0,1:T(8,128)}), f32[2048,64]{0,1:T(8,128)}) %all-reduce.3.cloned.1.call-update) | async-done | bytes 524304 | tf_op jit(solution)/shard_map/psum | solution.py:80
  204.4 1.8 multiply_reduce_fusion
  206.2 92.0 %all-reduce.5.cloned.1.call-done = f32[64,768]{1,0:T(8,128)} async-done(((f32[64,768]{1,0:T(8,128)}), f32[64,768]{1,0:T(8,128)}) %all-reduce.5.cloned.1.call-update) | async-done | bytes 196624 | tf_op jit(solution)/shard_map/psum | solution.py:81
  298.3 1.6 multiply_reduce_fusion.1
  299.9 11.2 %psum.22 = f32[]{:T(128)} all-reduce(f32[]{:T(128)} %multiply_reduce_fusion), channel_id=1, replica_groups=mesh['groups'=2,'fsdp'=4,'dp'=2,'pair'=2] {'fsdp'}, use_global_device_ids=true, to_apply=%region_5.6 | all-reduce | flops 1 | bytes 8 | tf_op jit(solution)/shard_map/psum | solution.py:82
  312.4 1.6 broadcast_multiply_fusion.1
  314.0 1.9 broadcast_multiply_fusion
  (4 shorter events, 0.1 us)
Async XLA Ops:
  7.2 32.0 %copy-start = (bf16[2048,768]{1,0:T(8,128)(2,1)S(1)}, bf16[2048,768]{1,0:T(8,128)(2,1)}, u32[]{:S(2)}) copy-start(bf16[2048,768]{1,0:T(8,128)(2,1)} %param.8) | copy-start | bytes 9437188
  7.2 24.3 %copy-start.3 = (bf16[128,768]{1,0:T(8,128)(2,1)S(1)}, bf16[128,768]{1,0:T(8,128)(2,1)}, u32[]{:S(2)}) copy-start(bf16[128,768]{1,0:T(8,128)(2,1)} %param.11) | copy-start | bytes 589828
  7.2 133.1 %reduce-scatter.2.cloned.1.call-start = ((), (), s32[]{:S(2)}) async-start(), calls=%async_computation.2 | async-start | bytes 2621440 | tf_op jit(solution)/shard_map/reduce_scatter | solution.py:76
  7.2 24.3 %collective-permute-start = (bf16[128,768]{1,0:T(8,128)(2,1)}, bf16[128,768]{1,0:T(8,128)(2,1)S(1)}, u32[]{:S(2)}, u32[]{:S(2)}) collective-permute-start(bf16[128,768]{1,0:T(8,128)(2,1)} %param.11), channel_id=1, source_target_pairs={{0,4},{4,8},{8,12},{12,0},{1,5},{5,9},{9,13},{13,1},{2,6},{6,10},{... | collective-permute-start | bytes 589832 | tf_op jit(solution)/shard_map/ppermute | solution.py:21
  10.3 22.5 %collective-permute-start.1 = (bf16[128,768]{1,0:T(8,128)(2,1)}, bf16[128,768]{1,0:T(8,128)(2,1)}, u32[]{:S(2)}, u32[]{:S(2)}) collective-permute-start(bf16[128,768]{1,0:T(8,128)(2,1)} %param.11), channel_id=1, source_target_pairs={{0,12},{4,0},{8,4},{12,8},{1,13},{5,1},{9,5},{13,9},{2,14},{6,2},{... | collective-permute-start | bytes 589832 | tf_op jit(solution)/shard_map/ppermute | solution.py:24
  31.6 7.5 %collective-permute-start.2 = (bf16[128,768]{1,0:T(8,128)(2,1)S(1)}, bf16[128,768]{1,0:T(8,128)(2,1)S(1)}, u32[]{:S(2)}, u32[]{:S(2)}) collective-permute-start(bf16[128,768]{1,0:T(8,128)(2,1)S(1)} %collective-permute-done), channel_id=1, source_target_pairs={{0,4},{4,8},{8,12},{12,0},{1,5},{5,9},{9,13},{13,1},{2,6},{6,10},{... | collective-permute-start | bytes 589832 | tf_op jit(solution)/shard_map/ppermute | solution.py:21
  91.4 2.5 copy-start.2
  91.4 2.4 copy-start.4
  91.9 1.9 copy-start.1
  97.3 72.0 %all-gather.2.cloned.1.call-start = ((), (), s32[]{:S(2)}) async-start(), calls=%async_computation.4 | async-start | bytes 1310720 | tf_op jit(solution)/shard_map/all_gather | solution.py:67
  98.0 106.4 %all-reduce.3.cloned.1.call-start = ((), (), s32[]{:S(2)}) async-start(), calls=%async_computation.3 | async-start | bytes 1048576 | tf_op jit(solution)/shard_map/psum | solution.py:80
  140.3 157.9 %all-reduce.5.cloned.1.call-start = ((), (), s32[]{:S(2)}) async-start(), calls=%async_computation.5 | async-start | bytes 393216 | tf_op jit(solution)/shard_map/psum | solution.py:81
Sparse Core Ops, SparseCore 0:
  97.4 42.8 reduce-scatter.1
  142.0 27.2 all-gather.1
  171.7 32.6 all-reduce.2
  208.7 89.5 all-reduce.4
